TPU v7x, 512 devices: a whole 4x8x8 slice. The times are simulated.
512 devices in a mesh: zone: 16 (over y, core), sub: 32 (over z, x).
Axes of the slice: x: 4, y: 8, z: 8, core: 2. Of those that a mesh axis runs over, the one named last changes fastest.
Arguments:
- diag_blocks: bfloat16 [16, 32, 2, 384, 384], P('zone', 'sub')
- precond_blocks: bfloat16 [16, 32, 2, 384, 384], P('zone', 'sub')
- offdiag_blocks: bfloat16 [16, 32, 2, 4, 384, 384], P('zone', 'sub'), may hold values from -0.09375 to 0.09375
- offdiag_col: int32 [16, 32, 2, 4], P('zone', 'sub'), may hold values from 1 to 10, as said below
- slot_live: int32 [16, 32, 2, 4], P('zone', 'sub'), may hold values from 0 to 1, as said below
- adjoint_rhs: bfloat16 [16, 32, 2, 384, 256], P('zone', 'sub'), may hold values from -6 to 6
- perf_cell: int32 [16, 32, 128], P('zone', 'sub'), may hold values from 0 to 255
- perf_well: int32 [16, 32, 128], P('zone', 'sub'), may hold values from 0 to 2047
- perf_coeff: float32 [16, 32, 3, 128], P('zone', 'sub'), may hold values from -4 to 4
Outputs:
- adjoint: float32 [16, 32, 2, 384, 256], P('zone', 'sub')
- well_gradient: float32 [2048, 256], P(('zone', 'sub'))
Inputs may be any that keep to these rules, and one draw needn't show every extreme that they name: `offdiag_col`: entry k of super-block b of a device is a position e of a grid of 3 rows and 4 columns around the device (row e // 4, column e % 4; the device's own super-block b at row 1, column b + 1). The 4 entries of super-block b name, in some order, its four neighbours: rows 0 and 2 at column b + 1, and row 1 at columns b and b + 2. `slot_live`: 1 wherever the neighbour named lies on another device.
All inputs are finite; a program needn't handle non-finite values.
Results may differ from a plain program's by a relative error of at most 0.0026.
Values may be sent and summed in bfloat16 or wider, within the bound.
A program may use at most 64 MiB of HBM per device.

v0:
```python
import jax
import jax.numpy as jnp
from jax import lax
from jax.sharding import PartitionSpec as P

ITERS = 3
WELL_DEV = 4


highest = lax.Precision.HIGHEST


def with_halo(cells, sides, width):
    for axis, dim in sides:
        count = lax.axis_size(axis)
        ends = count - 1
        head = lax.slice_in_dim(cells, 0, width, axis=dim)
        tail = lax.slice_in_dim(cells, cells.shape[dim] - width, cells.shape[dim], axis=dim)
        cells = jnp.concatenate(
            [
                lax.ppermute(tail, axis, [(i, (i + 1) % count) for i in range(ends)]),
                cells,
                lax.ppermute(head, axis, [((i + 1) % count, i) for i in range(ends)]),
            ],
            axis=dim,
        )
    return cells


def least_squares(columns, rhs_norm):
    count_cols = len(columns)
    basis = []
    triangle = [[None] * count_cols for unused in range(count_cols)]
    for column in range(count_cols):
        residue = columns[column]
        for earlier in range(column):
            weight = jnp.sum(basis[earlier] * columns[column], axis=0)
            triangle[earlier][column] = weight
            residue = residue - weight * basis[earlier]
        length = jnp.sqrt(jnp.sum(residue * residue, axis=0))
        triangle[column][column] = length
        basis.append(residue / length)
    solution = [None] * count_cols
    for column in reversed(range(count_cols)):
        summed = rhs_norm * basis[column][0]
        for later_col in range(column + 1, count_cols):
            summed = summed - triangle[column][later_col] * solution[later_col]
        solution[column] = summed / triangle[column][column]
    return solution


def local_inner(left_vec, right_vec):
    return jnp.sum(left_vec * right_vec, axis=(0, 1))


def shards(
    diag_blocks,
    precond_blocks,
    offdiag_blocks,
    offdiag_col,
    slot_live,
    adjoint_rhs,
    perf_cell,
    perf_well,
    perf_coeff,
):
    diagonal = diag_blocks[0, 0]
    precond = precond_blocks[0, 0]
    offdiag = offdiag_blocks[0, 0]
    col_ids = offdiag_col[0, 0]
    live_ids = slot_live[0, 0]
    right_side = adjoint_rhs[0, 0].astype(jnp.float32)
    bcount, order_size, width_rhs = right_side.shape
    grid_width = bcount + 2
    rhs_norm = jnp.sqrt(lax.psum(local_inner(right_side, right_side), ("zone", "sub")))
    krylov = [right_side / rhs_norm]
    searches = []
    columns = []
    for iteration in range(ITERS):
        search = jnp.einsum(
            "bij,bjr->bir",
            precond,
            krylov[-1].astype(jnp.bfloat16),
            preferred_element_type=jnp.float32,
        )
        searches.append(search)
        rounded = search.astype(jnp.bfloat16)
        extended = with_halo(rounded[None], (("zone", 0), ("sub", 1)), 1)
        flattened = extended.reshape(3 * grid_width, order_size, width_rhs)
        summed = jnp.einsum("bij,bjr->bir", diagonal, rounded, preferred_element_type=jnp.float32)
        picked = jnp.take(flattened, col_ids, axis=0)
        picked = jnp.where(live_ids[:, :, None, None] > 0, picked, jnp.zeros((), jnp.bfloat16))
        summed = summed + jnp.einsum(
            "bkij,bkjr->bir", offdiag, picked, preferred_element_type=jnp.float32
        )
        mapped = summed
        projected = jnp.stack([local_inner(earlier, mapped) for earlier in krylov])
        heights = lax.psum(projected, ("zone", "sub"))
        for position in range(len(krylov)):
            mapped = mapped - heights[position] * krylov[position]
        length = jnp.sqrt(lax.psum(local_inner(mapped, mapped), ("zone", "sub")))
        if iteration + 1 < ITERS:
            krylov.append(mapped / length)
        entries = (
            [heights[position] for position in range(iteration + 1)]
            + [length]
            + [jnp.zeros_like(length)] * (ITERS - 1 - iteration)
        )
        columns.append(jnp.stack(entries))
    solution = least_squares(columns, rhs_norm)
    adjoint = solution[0] * searches[0]
    for position in range(1, ITERS):
        adjoint = adjoint + solution[position] * searches[position]
    lam_rows = adjoint.reshape(bcount * order_size, width_rhs)
    cell_ids = perf_cell[0, 0]
    cell_size = order_size // 3
    row_index = (
        (cell_ids // cell_size * order_size)[None, :]
        + (jnp.arange(3, dtype=jnp.int32) * cell_size)[:, None]
        + (cell_ids % cell_size)[None, :]
    )
    picked_rows = jnp.take(lam_rows, row_index, axis=0)
    contrib = -jnp.einsum("kp,kpr->pr", perf_coeff[0, 0], picked_rows, precision=highest)
    well_ids = perf_well[0, 0]
    owners = jnp.arange(WELL_DEV * lax.axis_size(("zone", "sub")), dtype=jnp.int32)
    selector = (owners[:, None] == well_ids[None, :]).astype(jnp.float32)
    gradient = lax.psum_scatter(
        jnp.dot(selector, contrib, precision=highest),
        ("zone", "sub"),
        scatter_dimension=0,
        tiled=True,
    )
    return (adjoint[None, None], gradient)


def solution(mesh):
    placed = (
        P("zone", "sub", None, None, None),
        P("zone", "sub", None, None, None),
        P("zone", "sub", None, None, None, None),
        P("zone", "sub", None, None),
        P("zone", "sub", None, None),
        P("zone", "sub", None, None, None),
        P("zone", "sub", None),
        P("zone", "sub", None),
        P("zone", "sub", None, None),
    )
    return jax.shard_map(
        shards,
        mesh=mesh,
        in_specs=placed,
        out_specs=(P("zone", "sub", None, None, None), P(("zone", "sub"), None)),
        check_vma=False,
    )
```

profile of v0, /device:TPU:1, one launch (start us, length us, event | category | flops | bytes accessed | tf_op | source)
XLA Modules:
  0.0 1135.3 jit_solution(10928806940566803642)
XLA Ops:
  8.7 106.2 %psum.49 = f32[256]{0:T(256)S(1)} all-reduce(f32[256]{0:T(256)S(1)} %fusion.40), channel_id=1, replica_groups=mesh['zone'=16,'sub'=32] {'zone','sub'}, use_global_device_ids=true, to_apply=%region_1.0 | all-reduce | flops 256 | bytes 2048 | tf_op jit(solution)/shard_map/psum | solution.py:75
  114.9 1.6 fusion.57
  117.4 3.0 collective-permute-start
  120.3 2.1 collective-permute-start.1
  123.1 2.2 collective-permute-done
  125.4 4.4 collective-permute-done.1
  129.7 1.4 pad_maximum_fusion.3
  131.3 2.6 collective-permute-start.2
  137.1 5.1 collective-permute-done.2
  142.2 4.1 collective-permute-done.3
  146.3 2.7 pad_maximum_fusion
  149.1 3.6 gather_fusion.1
  152.7 2.7 multiply_reduce_fusion.8
  155.4 100.9 %psum.50 = f32[1,256]{1,0:T(1,128)S(1)} all-reduce(f32[1,256]{1,0:T(1,128)S(1)} %bitcast.197), channel_id=1, replica_groups=mesh['zone'=16,'sub'=32] {'zone','sub'}, use_global_device_ids=true, to_apply=%region_3.5 | all-reduce | flops 256 | bytes 2048 | tf_op jit(solution)/shard_map/psum | solution.py:98
  256.6 94.6 %psum.51 = f32[256]{0:T(256)} all-reduce(f32[256]{0:T(256)S(1)} %multiply_reduce_fusion.7), channel_id=1, replica_groups=mesh['zone'=16,'sub'=32] {'zone','sub'}, use_global_device_ids=true, to_apply=%region_5.7 | all-reduce | flops 256 | bytes 2048 | tf_op jit(solution)/shard_map/psum | solution.py:101
  353.1 3.4 collective-permute-start.4
  356.6 1.9 collective-permute-start.5
  358.5 2.7 collective-permute-done.4
  361.3 4.4 collective-permute-done.5
  366.0 4.1 collective-permute-start.6
  373.4 4.5 collective-permute-done.6
  377.9 4.1 collective-permute-done.7
  382.0 1.6 pad_maximum_fusion.1
  383.6 3.6 gather_fusion.2
  387.2 3.8 multiply_reduce_fusion.6
  391.7 102.9 %psum.52 = f32[2,256]{1,0:T(2,128)S(1)} all-reduce(f32[2,256]{1,0:T(2,128)} %pad_maximum_fusion.8), channel_id=1, replica_groups=mesh['zone'=16,'sub'=32] {'zone','sub'}, use_global_device_ids=true, to_apply=%region_9.11 | all-reduce | flops 512 | bytes 4096 | tf_op jit(solution)/shard_map/psum | solution.py:98
  494.6 3.2 multiply_reduce_fusion.4
  497.8 94.9 %psum.53 = f32[256]{0:T(256)} all-reduce(f32[256]{0:T(256)} %get-tuple-element.28), channel_id=1, replica_groups=mesh['zone'=16,'sub'=32] {'zone','sub'}, use_global_device_ids=true, to_apply=%region_11.13 | all-reduce | flops 256 | bytes 2048 | tf_op jit(solution)/shard_map/psum | solution.py:101
  593.4 1.8 fusion.53
  596.8 2.4 collective-permute-start.8
  599.3 2.6 collective-permute-start.9
  603.8 1.4 copy.28
  608.7 1.4 pad_maximum_fusion.5
  610.2 3.8 collective-permute-start.10
  618.7 7.4 collective-permute-done.10
  626.0 4.1 collective-permute-done.11
  630.2 2.7 pad_maximum_fusion.2
  632.9 3.7 gather_fusion.3
  636.6 4.2 multiply_reduce_fusion.3
  641.4 100.2 %psum.54 = f32[3,256]{1,0:T(4,128)S(1)} all-reduce(f32[3,256]{1,0:T(4,128)} %pad_maximum_fusion.6), channel_id=1, replica_groups=mesh['zone'=16,'sub'=32] {'zone','sub'}, use_global_device_ids=true, to_apply=%region_17.19 | all-reduce | flops 768 | bytes 6144 | tf_op jit(solution)/shard_map/psum | solution.py:98
  741.6 2.6 multiply_reduce_fusion
  744.2 94.7 %psum.55 = f32[256]{0:T(256)S(1)} all-reduce(f32[256]{0:T(256)} %multiply_reduce_fusion), channel_id=1, replica_groups=mesh['zone'=16,'sub'=32] {'zone','sub'}, use_global_device_ids=true, to_apply=%region_19.21 | all-reduce | flops 256 | bytes 2048 | tf_op jit(solution)/shard_map/psum | solution.py:101
  840.4 2.5 multiply_add_fusion
  842.8 1.4 copy.20
  844.3 1.7 gather_fusion
  846.1 2.1 fusion.60
  848.2 2.3 fusion.39
  852.8 274.4 %all-reduce.3.cloned.1.call-done = f32[2048,256]{1,0:T(8,128)} async-done(((f32[2048,256]{1,0:T(8,128)}), f32[2048,256]{1,0:T(8,128)}) %all-reduce.3.cloned.1.call-update) | async-done | bytes 2097168
  (124 shorter events, 30.9 us)
Async XLA Ops:
  7.2 145.5 %copy-start = (bf16[1,1,2,4,384,384]{5,4,3,2,1,0:T(8,128)(2,1)S(1)}, bf16[1,1,2,4,384,384]{5,4,3,2,1,0:T(8,128)(2,1)}, u32[]{:S(2)}) copy-start(bf16[1,1,2,4,384,384]{5,4,3,2,1,0:T(8,128)(2,1)} %param.13) | copy-start | bytes 7077892
  7.2 1120.0 %all-reduce.3.cloned.1.call-start = ((), (), s32[]{:S(2)}) async-start(), calls=%async_computation | async-start | bytes 4194304
  114.9 1.6 copy-start.20
  114.9 7.5 copy-start.28
  116.5 19.3 %copy-start.2 = (f32[2,256,384]{2,1,0:T(8,128)}, f32[2,256,384]{2,1,0:T(8,128)S(1)}, u32[]{:S(2)}) copy-start(f32[2,256,384]{2,1,0:T(8,128)S(1)} %fusion.57) | copy-start | bytes 2359300
  117.4 8.0 collective-permute-start
  120.3 9.4 collective-permute-start.1
  131.1 4.1 copy-start.30
  131.2 4.6 copy-start.6
  131.3 10.9 collective-permute-start.2
  133.9 12.4 %collective-permute-start.3 = (bf16[3,1,384,256]{2,3,1,0:T(8,128)(2,1)S(1)}, bf16[3,1,384,256]{2,3,1,0:T(8,128)(2,1)S(1)}, u32[]{:S(2)}, u32[]{:S(2)}) collective-permute-start(bf16[3,1,384,256]{2,3,1,0:T(8,128)(2,1)S(1)} %get-tuple-element.35), channel_id=1, source_target_pairs={{1,0},{2,1},{3,2},{4,3},{5,4},{6,5},{7,6},{8,7},{9,8},{10,9},{11,1... | collective-permute-start | bytes 1769480 | tf_op jit(solution)/shard_map/ppermute | solution.py:23
  135.2 248.4 %copy-start.15 = (s32[1024]{0:T(1024)}, s32[1024]{0:T(1024)S(1)}, u32[]{:S(2)}) copy-start(s32[1024]{0:T(1024)S(1)} %pad_clamp_fusion.1) | copy-start | bytes 12292
  149.0 3.6 copy-start.32
  351.2 1.1 copy-start.9
  351.9 254.5 %copy-start.10 = (f32[256]{0:T(256)}, f32[256]{0:T(256)S(1)}, u32[]{:S(2)}) copy-start(f32[256]{0:T(256)S(1)} %sqrt.40) | copy-start | bytes 3076
  352.3 0.9 copy-start.1
  352.3 6.2 copy-start.31
  353.1 8.1 collective-permute-start.4
  356.6 9.1 collective-permute-start.5
  358.5 12.9 %copy-start.24 = (s32[128]{0:T(128)}, s32[128]{0:T(128)S(1)}, u32[]{:S(2)}) copy-start(s32[128]{0:T(128)S(1)} %get-tuple-element.41) | copy-start | bytes 1540
  358.5 12.9 %copy-start.25 = (s32[128]{0:T(128)}, s32[128]{0:T(128)S(1)}, u32[]{:S(2)}) copy-start(s32[128]{0:T(128)S(1)} %get-tuple-element.42) | copy-start | bytes 1540
  365.8 6.3 copy-start.7
  366.0 11.9 %collective-permute-start.6 = (bf16[3,1,384,256]{2,3,1,0:T(8,128)(2,1)S(1)}, bf16[3,1,384,256]{2,3,1,0:T(8,128)(2,1)S(1)}, u32[]{:S(2)}, u32[]{:S(2)}) collective-permute-start(bf16[3,1,384,256]{2,3,1,0:T(8,128)(2,1)S(1)} %get-tuple-element.32), channel_id=1, source_target_pairs={{0,1},{1,2},{2,3},{3,4},{4,5},{5,6},{6,7},{7,8},{8,9},{9,10},{10,1... | collective-permute-start | bytes 1769480 | tf_op jit(solution)/shard_map/ppermute | solution.py:21
  370.1 11.9 %collective-permute-start.7 = (bf16[3,1,384,256]{2,3,1,0:T(8,128)(2,1)S(1)}, bf16[3,1,384,256]{2,3,1,0:T(8,128)(2,1)S(1)}, u32[]{:S(2)}, u32[]{:S(2)}) collective-permute-start(bf16[3,1,384,256]{2,3,1,0:T(8,128)(2,1)S(1)} %get-tuple-element.33), channel_id=1, source_target_pairs={{1,0},{2,1},{3,2},{4,3},{5,4},{6,5},{7,6},{8,7},{9,8},{10,9},{11,1... | collective-permute-start | bytes 1769480 | tf_op jit(solution)/shard_map/ppermute | solution.py:23
  371.4 6.5 copy-start.26
  593.4 1.8 copy-start.12
  593.4 8.6 copy-start.21
  595.2 0.9 copy-start.3
  596.8 10.2 collective-permute-start.8
  599.3 9.4 collective-permute-start.9
  607.1 0.6 copy-start.18
  610.1 5.3 copy-start.11
  610.1 5.3 copy-start.13
  610.1 5.3 copy-start.22
  610.1 5.3 copy-start.23
  610.1 7.2 copy-start.4
  610.1 7.2 copy-start.8
  610.2 15.8 %collective-permute-start.10 = (bf16[3,1,384,256]{2,3,1,0:T(8,128)(2,1)S(1)}, bf16[3,1,384,256]{2,3,1,0:T(8,128)(2,1)S(1)}, u32[]{:S(2)}, u32[]{:S(2)}) collective-permute-start(bf16[3,1,384,256]{2,3,1,0:T(8,128)(2,1)S(1)} %get-tuple-element.30), channel_id=1, source_target_pairs={{0,1},{1,2},{2,3},{3,4},{4,5},{5,6},{6,7},{7,8},{8,9},{9,10},{10,1... | collective-permute-start | bytes 1769480 | tf_op jit(solution)/shard_map/ppermute | solution.py:21
  614.1 16.1 %collective-permute-start.11 = (bf16[3,1,384,256]{2,3,1,0:T(8,128)(2,1)S(1)}, bf16[3,1,384,256]{2,3,1,0:T(8,128)(2,1)S(1)}, u32[]{:S(2)}, u32[]{:S(2)}) collective-permute-start(bf16[3,1,384,256]{2,3,1,0:T(8,128)(2,1)S(1)} %get-tuple-element.31), channel_id=1, source_target_pairs={{1,0},{2,1},{3,2},{4,3},{5,4},{6,5},{7,6},{8,7},{9,8},{10,9},{11,1... | collective-permute-start | bytes 1769480 | tf_op jit(solution)/shard_map/ppermute | solution.py:23
  615.5 10.5 copy-start.17
  616.7 9.3 copy-start.19
  632.9 3.7 copy-start.14
  842.8 1.4 copy-start.16
  844.2 1.7 copy-start.27
  844.3 3.9 copy-start.29
  850.5 1.1 copy-start.5
Sparse Core Ops, SparseCore 0:
  850.6 276.5 all-reduce.2
where the time goes:
time: 1140 us
  blocking collectives  694 us (61%)
  waiting for transfers between devices  319 us (28%)
  starting transfers between devices  30 us (3%)
  other arithmetic  28.5 us (2%)
  local copies, waits for them, and re-layouts  26.6 us (2%)
  matrix products  22.9 us (2%)
  between operations  14.6 us (1%)
    psum x3, blocking collectives, shards(): heights = lax.psum(projected, ('zone', 'sub'))  304 us
    psum x3, blocking collectives, shards(): length = jnp.sqrt(lax.psum(local_inner(mapped, mapped), ('zone', 'sub')))  284 us
    unnamed x2, waiting for transfers between devices  274 us
    psum x1, blocking collectives, shards(): lax.psum(local_inner(right_side, right_side), ('zone', 'sub'))  106 us
  transfers between devices with their start and end apart: 13, of which 12 were waited for; matrix products, arithmetic and copies ran while one was open for 1% of the time, Pallas kernels for 0%

commit v1 on v0

v1 whole, which is shorter than its diff:
```python
import functools

import jax
import jax.numpy as jnp
from jax import lax
from jax.experimental import pallas as pl
from jax.experimental.pallas import tpu as pltpu
from jax.sharding import PartitionSpec as P

MESH = pl.DeviceIdType.MESH
BF = jnp.bfloat16
F32 = jnp.float32
BLOCK = 384
ROWS = 768
R = 256
ITERS = 3
FAST, SLOW, SIDE = 0, 2, 4
RED_ROWS = (8, 16, 8)


def place():
    zone = lax.axis_index("zone")
    sub = lax.axis_index("sub")
    return zone, sub, zone // 2, lax.rem(zone, 2), sub // 4, lax.rem(sub, 4)


def group(name):
    zone, sub, y, core, z, x = place()
    if name == "xc":
        return 8, core * 4 + x, lambda i: (y * 2 + i // 4, z * 4 + lax.rem(i, 4))
    if name == "y":
        return 8, y, lambda i: (i * 2 + core, sub)
    if name == "z":
        return 8, z, lambda i: (zone, i * 4 + x)
    if name == "zone":
        return 16, zone, lambda i: (i, sub)
    if name == "sub":
        return 32, sub, lambda i: (zone, i)
    pair = sub // 2 * 2
    return 32, zone * 2 + lax.rem(sub, 2), lambda i: (i // 2, pair + lax.rem(i, 2))


def others(name):
    count, me, at = group(name)
    for step in range(1, count):
        slot = lax.rem(me + step, count)
        yield slot, at(slot)


def split(value):
    high = value.astype(BF)
    return high, (value - high.astype(F32)).astype(BF)


def dot(left, right):
    return jnp.dot(left, right, preferred_element_type=F32)


def fold(row):
    return [row[:, :128], row[:, 128:]]


def unfold(tile, position):
    return jnp.concatenate(
        [tile[2 * position : 2 * position + 1], tile[2 * position + 1 : 2 * position + 2]], axis=1
    )


def kernel(
    diag_hbm,
    pre_hbm,
    off_hbm,
    rhs_hbm,
    col_ref,
    live_ref,
    cell_ref,
    well_ref,
    coeff_ref,
    adj_hbm,
    grad_ref,
    diag,
    pre,
    off,
    rhs,
    search,
    image,
    high,
    low,
    near,
    far,
    side,
    red0,
    red1,
    red2,
    pick_high,
    pick_low,
    wells,
    lows,
    contrib,
    spread,
    dense,
    partial,
    piece,
    final,
    turned,
    out,
    load_sem,
    halo_send,
    halo_recv,
    red_send,
    red_recv,
    well_send,
    well_recv,
    store_sem,
):
    zone, sub, y, core, z, x = place()
    reds = (red0, red1, red2)

    loads = [
        pltpu.make_async_copy(src, dst, load_sem.at[i])
        for i, (src, dst) in enumerate(
            ((pre_hbm, pre), (rhs_hbm, rhs), (diag_hbm, diag), (off_hbm, off))
        )
    ]
    for load in loads:
        load.start()

    barrier = pltpu.get_barrier_semaphore()
    greeted = 0
    for name in ("zone", "sub", "pair", "xc"):
        for _, device in others(name):
            pl.semaphore_signal(barrier, inc=1, device_id=device, device_id_type=MESH)
            greeted += 1

    mate = (zone + 1 - 2 * core, sub)
    beyond = (zone - 1 + 2 * core, sub)
    has_far = jnp.logical_and(beyond[0] >= 0, beyond[0] < 16)
    has_side = (sub > 0, sub < 31)
    side_dev = ((zone, sub - 1), (zone, sub + 1))

    @pl.when(jnp.logical_not(has_far))
    def _():
        far[...] = jnp.zeros(far.shape, BF)

    for b in range(2):

        @pl.when(jnp.logical_not(has_side[b]))
        def _():
            side[:, b] = jnp.zeros((ITERS, BLOCK, R), BF)

    def halo(j, b):
        src = high.at[j, pl.ds(b * BLOCK, BLOCK)]
        every = []
        for kind, dst, device, sends, receives in (
            (SIDE, side.at[j, 1 - b], side_dev[b], has_side[b], has_side[1 - b]),
            (SLOW, far.at[j, b], beyond, has_far, has_far),
            (FAST, near.at[j, b], mate, None, None),
        ):
            copy = pltpu.make_async_remote_copy(
                src,
                dst,
                halo_send.at[j, kind + b],
                halo_recv.at[j, kind + b],
                device_id=device,
                device_id_type=MESH,
            )
            every.append((copy, sends, receives))
        return every

    def guarded(condition, action):
        if condition is None:
            action()
        else:
            pl.when(condition)(action)

    def halo_start(j, b):
        for copy, sends, _ in halo(j, b):
            guarded(sends, copy.start)

    def halo_wait(j, which):
        for b in range(2):
            copy, _, receives = halo(j, b)[which]
            guarded(receives, copy.wait_recv)

    def precondition(j, b, value):
        if j == 0:
            found = dot(pre[b], value)
        else:
            upper, lower = split(value)
            found = dot(pre[b], upper) + dot(pre[b], lower)
        rows = pl.ds(b * BLOCK, BLOCK)
        search[j, rows] = found
        upper, lower = split(found)
        high[j, rows] = upper
        low[j, rows] = lower

    def slot_of(b, position):
        where = 0
        for k in range(1, 4):
            where = where + jnp.where(col_ref[b, k] == position, k, 0)
        return b * 4 + where

    def live_of(b, position):
        found = 0
        for k in range(4):
            found = found + jnp.where(col_ref[b, k] == position, live_ref[b, k], 0)
        return found

    def local_products(j):
        for b in range(2):
            mine = pl.ds(b * BLOCK, BLOCK)
            other = pl.ds((1 - b) * BLOCK, BLOCK)
            total = dot(diag[b], high[j, mine]) + dot(diag[b], low[j, mine])
            block = off[slot_of(b, 6 - b)]
            inner = dot(block, high[j, other]) + dot(block, low[j, other])
            image[j, mine] = total + jnp.where(live_of(b, 6 - b) > 0, inner, 0.0)

    def halo_products(j):
        halo_wait(j, 2)
        for b in range(2):
            position = jnp.where(core == 0, 9 + b, 1 + b)
            image[j, pl.ds(b * BLOCK, BLOCK)] += dot(off[slot_of(b, position)], near[j, b])
        halo_wait(j, 0)
        for b in range(2):
            image[j, pl.ds(b * BLOCK, BLOCK)] += dot(off[slot_of(b, 4 + 3 * b)], side[j, b])
        halo_wait(j, 1)
        for b in range(2):
            position = jnp.where(core == 0, 1 + b, 9 + b)
            image[j, pl.ds(b * BLOCK, BLOCK)] += dot(off[slot_of(b, position)], far[j, b])

    stages = ("xc", "y", "z")

    def red_start(which, stage, value):
        buf = reds[which].at[stage]
        _, me, _ = group(stages[stage])
        buf[me] = value
        for _, device in others(stages[stage]):
            pltpu.make_async_remote_copy(
                buf.at[me],
                buf.at[me],
                red_send.at[which, stage],
                red_recv.at[which, stage],
                device_id=device,
                device_id_type=MESH,
            ).start()

    def red_finish(which, stage):
        buf = reds[which].at[stage]
        seven = buf.at[pl.ds(0, 7)]
        pltpu.make_async_copy(seven, seven, red_recv.at[which, stage]).wait()
        total = buf[0]
        for i in range(1, 8):
            total = total + buf[i]
        if which == 0:
            largest = buf[0]
            for i in range(1, 8):
                largest = jnp.maximum(largest, buf[i])
            row = lax.broadcasted_iota(jnp.int32, total.shape, 0)
            total = jnp.where(row < 2, total, largest)
        return total

    def inner_products(makers, pairs):
        step = 64

        def body(i, sums):
            rows = pl.ds(pl.multiple_of(i * step, step), step)
            vectors = [make(rows) for make in makers]
            return tuple(
                total + jnp.sum((vectors[a] * vectors[c]).reshape(step // 8, 8, R), axis=0)
                for total, (a, c) in zip(sums, pairs)
            )

        sums = lax.fori_loop(
            0, ROWS // step, body, tuple(jnp.zeros((8, R), F32) for _ in pairs)
        )
        return [jnp.sum(total, axis=0, keepdims=True) for total in sums]

    def payload(values, rows):
        pieces = [half for value in values for half in fold(value)]
        if len(pieces) < rows:
            pieces.append(jnp.zeros((rows - len(pieces), 128), F32))
        return jnp.concatenate(pieces, axis=0)

    def largest_of(ref, count):
        def body(i, best):
            return jnp.maximum(best, jnp.max(jnp.abs(ref[i].astype(F32).reshape(48, 8, BLOCK)), axis=0))

        best = lax.fori_loop(0, count, body, jnp.zeros((8, BLOCK), F32))
        return jnp.max(jnp.max(best, axis=0, keepdims=True), axis=1, keepdims=True)

    def wells_start():
        wells[zone] = well_ref[...]
        for _, device in others("zone"):
            pltpu.make_async_remote_copy(
                wells.at[zone],
                wells.at[zone],
                well_send.at[3],
                well_recv.at[3],
                device_id=device,
                device_id_type=MESH,
            ).start()

    def pick_build():
        cells = cell_ref[...]
        for b in range(2):
            for q in range(3):
                row = lax.broadcasted_iota(jnp.int32, (128, 128), 0) + b * 128
                value = jnp.where(row == cells, -coeff_ref[q : q + 1, :], 0.0)
                upper, lower = split(value)
                rows = pl.ds(b * BLOCK + q * 128, 128)
                pick_high[rows] = upper
                pick_low[rows] = lower

    def lows_build():
        fifteen = wells.at[pl.ds(0, 15)]
        pltpu.make_async_copy(fifteen, fifteen, well_recv.at[3]).wait()

        def body(i, carry):
            ids = wells[i]
            code = ((ids >> 7) << 3) + (ids & 7)
            row = lax.broadcasted_iota(jnp.int32, (128, 128), 0)
            lows[i] = jnp.where(row == code, 1.0, 0.0).astype(BF)
            return carry

        lax.fori_loop(0, 16, body, 0)

    def turned_dot(left, right):
        return lax.dot_general(left, right, (((0,), (0,)), ((), ())), preferred_element_type=F32)

    def contrib_start(j):
        value = (
            turned_dot(high[j], pick_high[...])
            + turned_dot(low[j], pick_high[...])
            + turned_dot(high[j], pick_low[...])
        )
        contrib[j] = value.reshape(16, 16, 128)
        spread[j, zone] = contrib[j, zone]
        for slot, device in others("zone"):
            pltpu.make_async_remote_copy(
                contrib.at[j, slot],
                spread.at[j, zone],
                well_send.at[j],
                well_recv.at[j],
                device_id=device,
                device_id_type=MESH,
            ).start()

    def dense_start(j):
        fifteen = spread.at[j, pl.ds(0, 15)]
        pltpu.make_async_copy(fifteen, fifteen, well_recv.at[j]).wait()

        def body(i, total):
            chunk = (wells[i] >> 3) & 15
            value = spread[j, i]
            placed = jnp.concatenate([jnp.where(chunk == k, value, 0.0) for k in range(16)], axis=0)
            upper, lower = split(placed)
            return total + lax.dot_general(
                jnp.concatenate([upper, lower], axis=0),
                lows[i],
                (((1,), (1,)), ((), ())),
                preferred_element_type=F32,
            )

        total = lax.fori_loop(0, 16, body, jnp.zeros((512, 128), F32))
        dense[j] = (total[:256] + total[256:]).reshape(32, 8, 128)
        partial[j, sub] = dense[j, sub]
        for slot, device in others("sub"):
            pltpu.make_async_remote_copy(
                dense.at[j, slot],
                partial.at[j, sub],
                well_send.at[4 + j],
                well_recv.at[4 + j],
                device_id=device,
                device_id_type=MESH,
            ).start()

    def dense_finish(j):
        most = partial.at[j, pl.ds(0, 31)]
        pltpu.make_async_copy(most, most, well_recv.at[4 + j]).wait()
        total = partial[j, 0]
        for i in range(1, 32):
            total = total + partial[j, i]
        piece[j] = total

    loads[0].wait()
    loads[1].wait()
    for b in range(2):
        precondition(0, b, rhs[pl.ds(b * BLOCK, BLOCK)])
    right_side = lambda rows: rhs[rows].astype(F32)
    (square,) = inner_products([right_side], [(0, 0)])
    pick_build()
    loads[2].wait()
    loads[3].wait()
    pl.semaphore_wait(barrier, greeted)
    for b in range(2):
        halo_start(0, b)
    wells_start()
    size_pre = largest_of(pre, 2)
    size_op = jnp.maximum(largest_of(diag, 2), largest_of(off, 8))
    red_start(
        0,
        0,
        jnp.concatenate(
            fold(square)
            + [
                jnp.broadcast_to(size_pre, (1, 128)),
                jnp.broadcast_to(size_op, (1, 128)),
                jnp.zeros((4, 128), F32),
            ],
            axis=0,
        ),
    )
    contrib_start(0)
    local_products(0)
    red_start(0, 1, red_finish(0, 0))
    halo_products(0)

    for b in range(2):
        precondition(1, b, image[0, pl.ds(b * BLOCK, BLOCK)])
        halo_start(1, b)
    contrib_start(1)
    local_products(1)
    red_start(0, 2, red_finish(0, 1))
    lows_build()
    dense_start(0)
    halo_products(1)

    sizes = red_finish(0, 2)
    rhs_norm = jnp.sqrt(unfold(sizes, 0))
    inverse = 1.0 / rhs_norm
    shrink = 1.0 / (
        jnp.concatenate([sizes[2:3], sizes[2:3]], axis=1)
        * jnp.concatenate([sizes[3:4], sizes[3:4]], axis=1)
    )
    scale1 = inverse * shrink
    for b in range(2):
        precondition(2, b, image[1, pl.ds(b * BLOCK, BLOCK)] * scale1)
        halo_start(2, b)
    unit = lambda rows: rhs[rows].astype(F32) * inverse
    first = lambda rows: image[0, rows] * inverse
    second = lambda rows: image[1, rows] * scale1
    third = lambda rows: image[2, rows] * shrink
    early = inner_products([unit, first, second], [(0, 1), (0, 2), (1, 1), (1, 2), (2, 2)])
    red_start(1, 0, payload(early, 16))
    contrib_start(2)
    local_products(2)
    red_start(1, 1, red_finish(1, 0))
    dense_start(1)
    halo_products(2)

    late = inner_products([unit, first, second, third], [(0, 3), (1, 3), (2, 3), (3, 3)])
    red_start(2, 0, payload(late, 8))
    dense_start(2)
    red_start(2, 1, red_finish(2, 0))
    red_start(1, 2, red_finish(1, 1))
    dense_finish(0)
    dense_finish(1)
    red_start(2, 2, red_finish(2, 1))
    head = red_finish(1, 2)
    g0, g1, m00, m01, m11 = [unfold(head, i) for i in range(5)]
    dense_finish(2)
    tail = red_finish(2, 2)
    g2, m02, m12, m22 = [unfold(tail, i) for i in range(4)]

    e01 = m01 / m00
    e02 = m02 / m00
    p11 = m11 - e01 * m01
    p12 = m12 - e01 * m02
    e12 = p12 / p11
    p22 = m22 - e02 * m02 - e12 * p12
    f0 = g0
    f1 = g1 - e01 * f0
    f2 = g2 - e02 * f0 - e12 * f1
    c2 = f2 / p22
    c1 = f1 / p11 - e12 * c2
    c0 = f0 / m00 - e01 * c1 - e02 * c2
    coeffs = [c0, c1 * shrink, c2 * shrink * rhs_norm]

    lane = lax.broadcasted_iota(jnp.int32, (8, R), 1)
    row = lax.broadcasted_iota(jnp.int32, (8, R), 0)
    mine = lane == row + (zone * 16 + lax.rem(sub, 2) * 8)
    tile = jnp.zeros((8, 128), F32)
    for j in range(ITERS):
        factor = jnp.sum(jnp.where(mine, coeffs[j], 0.0), axis=1, keepdims=True)
        tile = tile + factor * piece[j]
    _, me, _ = group("pair")
    final[me] = tile
    for _, device in others("pair"):
        pltpu.make_async_remote_copy(
            final.at[me],
            final.at[me],
            well_send.at[7],
            well_recv.at[7],
            device_id=device,
            device_id_type=MESH,
        ).start()

    stores = []
    for b in range(2):
        for half in range(2):
            rows = pl.ds(b * BLOCK + half * 192, 192)
            total = coeffs[0] * search[0, rows]
            for j in range(1, ITERS):
                total = total + coeffs[j] * search[j, rows]
            out[rows] = total
            store = pltpu.make_async_copy(out.at[rows], adj_hbm.at[rows], store_sem.at[b * 2 + half])
            store.start()
            stores.append(store)

    most = final.at[pl.ds(0, 31)]
    pltpu.make_async_copy(most, most, well_recv.at[7]).wait()
    gathered = final[...].reshape(R, 128)
    turned[...] = jnp.concatenate([gathered[:128].T, gathered[128:].T], axis=1)
    eight = turned[pl.ds(pl.multiple_of(zone * 8, 8), 8)]
    grad_ref[...] = jnp.where(lax.rem(sub, 2) == 0, eight[:4], eight[4:])

    for store in stores:
        store.wait()
    for j in range(ITERS):
        for b in range(2):
            for copy, sends, _ in halo(j, b):
                guarded(sends, copy.wait_send)
    for which in range(3):
        for stage in range(3):
            seven = reds[which].at[stage, pl.ds(0, 7)]
            pltpu.make_async_copy(seven, seven, red_send.at[which, stage]).wait()
    for j in range(ITERS):
        fifteen = spread.at[j, pl.ds(0, 15)]
        pltpu.make_async_copy(fifteen, fifteen, well_send.at[j]).wait()
        most = partial.at[j, pl.ds(0, 31)]
        pltpu.make_async_copy(most, most, well_send.at[4 + j]).wait()
    fifteen = wells.at[pl.ds(0, 15)]
    pltpu.make_async_copy(fifteen, fifteen, well_send.at[3]).wait()
    most = final.at[pl.ds(0, 31)]
    pltpu.make_async_copy(most, most, well_send.at[7]).wait()


def shards(
    diag_blocks,
    precond_blocks,
    offdiag_blocks,
    offdiag_col,
    slot_live,
    adjoint_rhs,
    perf_cell,
    perf_well,
    perf_coeff,
):
    any_spec = pl.BlockSpec(memory_space=pl.ANY)
    smem = pl.BlockSpec(memory_space=pltpu.SMEM)
    vmem = pl.BlockSpec(memory_space=pltpu.VMEM)
    dma = pltpu.SemaphoreType.DMA
    adjoint, gradient = pl.pallas_call(
        kernel,
        out_shape=(
            jax.ShapeDtypeStruct((ROWS, R), F32),
            jax.ShapeDtypeStruct((4, R), F32),
        ),
        in_specs=[any_spec] * 4 + [smem] * 2 + [vmem] * 3,
        out_specs=(any_spec, vmem),
        scratch_shapes=[
            pltpu.VMEM((2, BLOCK, BLOCK), BF),
            pltpu.VMEM((2, BLOCK, BLOCK), BF),
            pltpu.VMEM((8, BLOCK, BLOCK), BF),
            pltpu.VMEM((ROWS, R), BF),
            pltpu.VMEM((ITERS, ROWS, R), F32),
            pltpu.VMEM((ITERS, ROWS, R), F32),
            pltpu.VMEM((ITERS, ROWS, R), BF),
            pltpu.VMEM((ITERS, ROWS, R), BF),
            pltpu.VMEM((ITERS, 2, BLOCK, R), BF),
            pltpu.VMEM((ITERS, 2, BLOCK, R), BF),
            pltpu.VMEM((ITERS, 2, BLOCK, R), BF),
            pltpu.VMEM((3, 8, 8, 128), F32),
            pltpu.VMEM((3, 8, 16, 128), F32),
            pltpu.VMEM((3, 8, 8, 128), F32),
            pltpu.VMEM((ROWS, 128), BF),
            pltpu.VMEM((ROWS, 128), BF),
            pltpu.VMEM((16, 1, 128), jnp.int32),
            pltpu.VMEM((16, 128, 128), BF),
            pltpu.VMEM((ITERS, 16, 16, 128), F32),
            pltpu.VMEM((ITERS, 16, 16, 128), F32),
            pltpu.VMEM((ITERS, 32, 8, 128), F32),
            pltpu.VMEM((ITERS, 32, 8, 128), F32),
            pltpu.VMEM((ITERS, 8, 128), F32),
            pltpu.VMEM((32, 8, 128), F32),
            pltpu.VMEM((128, R), F32),
            pltpu.VMEM((ROWS, R), F32),
            dma((4,)),
            dma((ITERS, 6)),
            dma((ITERS, 6)),
            dma((3, 3)),
            dma((3, 3)),
            dma((8,)),
            dma((8,)),
            dma((4,)),
        ],
        compiler_params=pltpu.CompilerParams(
            collective_id=0, has_side_effects=True, vmem_limit_bytes=44 * 1024 * 1024
        ),
        name="adjoint_solve",
    )(
        diag_blocks.reshape(2, BLOCK, BLOCK),
        precond_blocks.reshape(2, BLOCK, BLOCK),
        offdiag_blocks.reshape(8, BLOCK, BLOCK),
        adjoint_rhs.reshape(ROWS, R),
        offdiag_col.reshape(2, 4),
        slot_live.reshape(2, 4),
        perf_cell.reshape(1, 128),
        perf_well.reshape(1, 128),
        perf_coeff.reshape(3, 128),
    )
    return adjoint.reshape(1, 1, 2, BLOCK, R), gradient


def solution(mesh):
    placed = (
        P("zone", "sub", None, None, None),
        P("zone", "sub", None, None, None),
        P("zone", "sub", None, None, None, None),
        P("zone", "sub", None, None),
        P("zone", "sub", None, None),
        P("zone", "sub", None, None, None),
        P("zone", "sub", None),
        P("zone", "sub", None),
        P("zone", "sub", None, None),
    )
    return jax.shard_map(
        shards,
        mesh=mesh,
        in_specs=placed,
        out_specs=(P("zone", "sub", None, None, None), P(("zone", "sub"), None)),
        check_vma=False,
    )
```

time: 1140 us -> 78.8 us (0.07)
  blocking collectives: 694 us -> 0 us
  waiting for transfers between devices: 319 us -> 0 us
  Pallas kernels: 0 us -> 68.2 us
  starting transfers between devices: 30 us -> 0 us
  other arithmetic: 28.5 us -> 0 us
  matrix products: 22.9 us -> 0 us
  local copies, waits for them, and re-layouts: 26.6 us -> 9.61 us
  between operations: 14.6 us -> 0.65 us
    psum x7 -> x0, blocking collectives: 694 us -> none  [the longest x3 304 us: shards(): heights = lax.psum(projected, ('zone', 'sub'))]
    unnamed x2 -> x0, waiting for transfers between devices: 274 us -> none
    pallas_call x0 -> x1, Pallas kernels: none -> 68.2 us  [shards(): pl.pallas_call(kernel, out_shape=(jax.ShapeDtypeStruct((ROWS, R), F32), j...]
    ppermute x12 -> x0, waiting for transfers between devices: 44.1 us -> none  [the longest x6 22.2 us: with_halo(): lax.ppermute(head, axis, [((i + 1) % count, i) for i in range(ends)])]
    ppermute x12 -> x0, starting transfers between devices: 29.9 us -> none  [the longest x6 19.4 us: with_halo(): lax.ppermute(tail, axis, [(i, (i + 1) % count) for i in range(ends)])]
    dot_general x11 -> x0, matrix products: 22.9 us -> none  [the longest x3 10.8 us: shards(): jnp.einsum('bkij,bkjr->bir', offdiag, picked, preferred_element_type=jnp....]
    gather x4 -> x0, local copies, waits for them, and re-layouts: 12.6 us -> none  [the longest x3 10.9 us: shards(): picked = jnp.take(flattened, col_ids, axis=0)]
  transfers between devices with their start and end apart: 13 -> 0, of which waited for: 12 -> 0; matrix products, arithmetic and copies ran while one was open for 1% -> 0% of each run, Pallas kernels for 0% -> 0%
where the time goes in v1:
time: 78.8 us; the launch traced here: 78.5 us
  Pallas kernels  68.2 us (87%)
  local copies, waits for them, and re-layouts  9.61 us (12%)
    pallas_call x1, Pallas kernels, shards(): pl.pallas_call(kernel, out_shape=(jax.ShapeDtypeStruct((ROWS, R), F32), j...  68.2 us
    unnamed x19, local copies, waits for them, and re-layouts  9.61 us

profile of v1, /device:TPU:1, one launch (start us, length us, event | category | flops | bytes accessed | tf_op | source)
XLA Modules:
  0.0 78.5 jit_solution(15807062553783594294)
XLA Ops:
  0.6 0.7 copy.13
  1.3 0.0 copy-start
  1.3 1.7 %copy-done = bf16[1,1,2,4,384,384]{5,4,3,2,1,0:T(8,128)(2,1)S(1)} copy-done((bf16[1,1,2,4,384,384]{5,4,3,2,1,0:T(8,128)(2,1)S(1)}, bf16[1,1,2,4,384,384]{5,4,3,2,1,0:T(8,128)(2,1)}, u32[]{:S(2)}) %copy-start) | copy-done | bytes 2359320
  3.0 0.0 copy-start.1
  3.0 1.1 %copy-done.1 = bf16[1,1,2,384,384]{4,3,2,1,0:T(8,128)(2,1)S(1)} copy-done((bf16[1,1,2,384,384]{4,3,2,1,0:T(8,128)(2,1)S(1)}, bf16[1,1,2,384,384]{4,3,2,1,0:T(8,128)(2,1)}, u32[]{:S(2)}) %copy-start.1) | copy-done | bytes 589848
  4.0 0.0 copy-start.2
  4.0 1.1 %copy-done.2 = bf16[1,1,2,384,384]{4,3,2,1,0:T(8,128)(2,1)S(1)} copy-done((bf16[1,1,2,384,384]{4,3,2,1,0:T(8,128)(2,1)S(1)}, bf16[1,1,2,384,384]{4,3,2,1,0:T(8,128)(2,1)}, u32[]{:S(2)}) %copy-start.2) | copy-done | bytes 589848
  5.1 0.0 copy-start.3
  5.1 1.0 %copy-done.3 = bf16[1,1,2,384,256]{4,3,2,1,0:T(8,128)(2,1)S(1)} copy-done((bf16[1,1,2,384,256]{4,3,2,1,0:T(8,128)(2,1)S(1)}, bf16[1,1,2,384,256]{4,3,2,1,0:T(8,128)(2,1)}, u32[]{:S(2)}) %copy-start.3) | copy-done | bytes 393240
  6.1 0.0 copy-start.4
  6.1 0.7 copy-done.4
  6.8 0.0 copy-start.5
  6.8 0.7 copy-done.5
  7.5 0.0 copy-start.6
  7.5 0.7 copy-done.6
  8.1 0.0 copy-start.7
  8.1 0.7 copy-done.7
  8.8 68.2 %adjoint_solve.1 = (f32[768,256]{1,0:T(8,128)S(1)}, f32[4,256]{1,0:T(4,128)S(1)}) custom-call(bf16[2,384,384]{2,1,0:T(8,128)(2,1)S(1)} %bitcast.14, bf16[2,384,384]{2,1,0:T(8,128)(2,1)S(1)} %bitcast.15, bf16[8,384,384]{2,1,0:T(8,128)(2,1)S(1)} %bitcast.12, bf16[768,256]{1,0:T(8,128)(2,1)S(1)} %bitcast.16, s32[2,4]{1,0:T(2,128)S(1)} %bitcast.18, ...), custom_call_target="tpu_custom_call" | custom-call | tf_op jit(solution)/shard_map/adjoint_solve/pallas_call | solution.py:553
  77.0 0.9 %copy.16 = f32[1,1,2,384,256]{4,3,2,1,0:T(8,128)} copy(f32[1,1,2,384,256]{4,3,2,1,0:T(8,128)S(1)} %bitcast.13) | data formatting | bytes 1572864
  77.9 0.6 copy.17
Async XLA Ops:
  1.3 1.7 %copy-start = (bf16[1,1,2,4,384,384]{5,4,3,2,1,0:T(8,128)(2,1)S(1)}, bf16[1,1,2,4,384,384]{5,4,3,2,1,0:T(8,128)(2,1)}, u32[]{:S(2)}) copy-start(bf16[1,1,2,4,384,384]{5,4,3,2,1,0:T(8,128)(2,1)} %param.11) | copy-start | bytes 7077892
  3.0 1.1 %copy-start.1 = (bf16[1,1,2,384,384]{4,3,2,1,0:T(8,128)(2,1)S(1)}, bf16[1,1,2,384,384]{4,3,2,1,0:T(8,128)(2,1)}, u32[]{:S(2)}) copy-start(bf16[1,1,2,384,384]{4,3,2,1,0:T(8,128)(2,1)} %param.9) | copy-start | bytes 1769476
  4.0 1.1 %copy-start.2 = (bf16[1,1,2,384,384]{4,3,2,1,0:T(8,128)(2,1)S(1)}, bf16[1,1,2,384,384]{4,3,2,1,0:T(8,128)(2,1)}, u32[]{:S(2)}) copy-start(bf16[1,1,2,384,384]{4,3,2,1,0:T(8,128)(2,1)} %param.10) | copy-start | bytes 1769476
  5.1 1.0 %copy-start.3 = (bf16[1,1,2,384,256]{4,3,2,1,0:T(8,128)(2,1)S(1)}, bf16[1,1,2,384,256]{4,3,2,1,0:T(8,128)(2,1)}, u32[]{:S(2)}) copy-start(bf16[1,1,2,384,256]{4,3,2,1,0:T(8,128)(2,1)} %param.14) | copy-start | bytes 1179652
  6.1 0.7 copy-start.4
  6.8 0.7 copy-start.5
  7.5 0.7 copy-start.6
  8.1 0.7 copy-start.7

commit v2 on v1

v2 whole, which is shorter than its diff:
```python
import functools

import jax
import jax.numpy as jnp
from jax import lax
from jax.experimental import pallas as pl
from jax.experimental.pallas import tpu as pltpu
from jax.sharding import PartitionSpec as P

MESH = pl.DeviceIdType.MESH
BF = jnp.bfloat16
F32 = jnp.float32
BLOCK = 384
ROWS = 768
R = 256
ITERS = 3
OFF_MOST = 0.09375
FAST, SLOW, SIDE = 0, 2, 4
RED_ROWS = (8, 16, 8)


def place():
    zone = lax.axis_index("zone")
    sub = lax.axis_index("sub")
    return zone, sub, zone // 2, lax.rem(zone, 2), sub // 4, lax.rem(sub, 4)


def group(name):
    zone, sub, y, core, z, x = place()
    if name == "xc":
        return 8, core * 4 + x, lambda i: (y * 2 + i // 4, z * 4 + lax.rem(i, 4))
    if name == "y":
        return 8, y, lambda i: (i * 2 + core, sub)
    if name == "z":
        return 8, z, lambda i: (zone, i * 4 + x)
    if name == "zone":
        return 16, zone, lambda i: (i, sub)
    if name == "sub":
        return 32, sub, lambda i: (zone, i)
    pair = sub // 2 * 2
    return 32, zone * 2 + lax.rem(sub, 2), lambda i: (i // 2, pair + lax.rem(i, 2))


def others(name):
    count, me, at = group(name)
    for step in range(1, count):
        slot = lax.rem(me + step, count)
        yield slot, at(slot)


def split(value):
    high = value.astype(BF)
    return high, (value - high.astype(F32)).astype(BF)


def dot(left, right):
    return jnp.dot(left, right, preferred_element_type=F32)


def kernel(
    diag_hbm,
    pre_hbm,
    off_hbm,
    rhs_hbm,
    col_ref,
    live_ref,
    cell_ref,
    well_ref,
    coeff_ref,
    adj_hbm,
    grad_ref,
    diag,
    pre,
    off,
    rhs,
    search,
    image,
    high,
    low,
    near,
    far,
    side,
    red0,
    red1,
    red2,
    pick,
    wells,
    lows,
    hots,
    contrib,
    spread,
    placed,
    dense,
    partial,
    final,
    turned,
    out,
    load_sem,
    halo_send,
    halo_recv,
    red_send,
    red_recv,
    well_send,
    well_recv,
    store_sem,
):
    zone, sub, y, core, z, x = place()
    reds = (red0, red1, red2)

    loads = [
        pltpu.make_async_copy(src, dst, load_sem.at[i])
        for i, (src, dst) in enumerate(
            ((pre_hbm, pre), (rhs_hbm, rhs), (diag_hbm, diag), (off_hbm, off))
        )
    ]
    for load in loads:
        load.start()

    barrier = pltpu.get_barrier_semaphore()
    greeted = 0
    for name in ("zone", "sub", "pair", "xc"):
        for _, device in others(name):
            pl.semaphore_signal(barrier, inc=1, device_id=device, device_id_type=MESH)
            greeted += 1

    mate = (zone + 1 - 2 * core, sub)
    beyond = (zone - 1 + 2 * core, sub)
    has_far = jnp.logical_and(beyond[0] >= 0, beyond[0] < 16)
    has_side = (sub > 0, sub < 31)
    side_dev = ((zone, sub - 1), (zone, sub + 1))

    @pl.when(jnp.logical_not(has_far))
    def _():
        far[...] = jnp.zeros(far.shape, BF)

    for b in range(2):

        @pl.when(jnp.logical_not(has_side[b]))
        def _():
            side[:, :, b] = jnp.zeros((ITERS, 2, BLOCK, 128), BF)

    def halo(j, h, kind, b):
        src = high.at[j, h, pl.ds(b * BLOCK, BLOCK)]
        dst, device, sends, receives = {
            SIDE: (side.at[j, h, 1 - b], side_dev[b], has_side[b], has_side[1 - b]),
            SLOW: (far.at[j, h, b], beyond, has_far, has_far),
            FAST: (near.at[j, h, b], mate, None, None),
        }[kind]
        copy = pltpu.make_async_remote_copy(
            src,
            dst,
            halo_send.at[j, h, kind + b],
            halo_recv.at[j, h, kind + b],
            device_id=device,
            device_id_type=MESH,
        )
        return copy, sends, receives

    def guarded(condition, action):
        if condition is None:
            action()
        else:
            pl.when(condition)(action)

    def halo_start(j, h):
        for b in range(2):
            for kind in (SLOW, SIDE, FAST):
                copy, sends, _ = halo(j, h, kind, b)
                guarded(sends, copy.start)

    def halo_wait(j, h, kind):
        for b in range(2):
            copy, _, receives = halo(j, h, kind, b)
            guarded(receives, copy.wait_recv)

    def keep(j, h, b, found):
        rows = pl.ds(b * BLOCK, BLOCK)
        search[j, h, rows] = found
        upper, lower = split(found)
        high[j, h, rows] = upper
        low[j, h, rows] = lower

    def both(left, upper, lower):
        found = dot(left, jnp.concatenate([upper, lower], axis=1))
        return found[:, :128] + found[:, 128:]

    def precondition(j, h, scale):
        for b in range(2):
            upper, lower = split(image[j - 1, h, pl.ds(b * BLOCK, BLOCK)])
            found = both(pre[b], upper, lower)
            keep(j, h, b, found if scale is None else found * scale())

    def slot_of(b, position):
        where = 0
        for k in range(1, 4):
            where = where + jnp.where(col_ref[b, k] == position, k, 0)
        return b * 4 + where

    def live_of(b, position):
        found = 0
        for k in range(4):
            found = found + jnp.where(col_ref[b, k] == position, live_ref[b, k], 0)
        return found

    def local_products(j, h):
        for b in range(2):
            mine = pl.ds(b * BLOCK, BLOCK)
            other = pl.ds((1 - b) * BLOCK, BLOCK)
            total = both(diag[b], high[j, h, mine], low[j, h, mine])
            inner = both(off[slot_of(b, 6 - b)], high[j, h, other], low[j, h, other])
            image[j, h, mine] = total + jnp.where(live_of(b, 6 - b) > 0, inner, 0.0)

    def halo_products(j, h):
        def add(b, position, block):
            image[j, h, pl.ds(b * BLOCK, BLOCK)] += dot(off[slot_of(b, position)], block)

        halo_wait(j, h, FAST)
        for b in range(2):
            add(b, jnp.where(core == 0, 9 + b, 1 + b), near[j, h, b])
        halo_wait(j, h, SIDE)
        for b in range(2):
            add(b, 4 + 3 * b, side[j, h, b])
        halo_wait(j, h, SLOW)
        for b in range(2):
            add(b, jnp.where(core == 0, 1 + b, 9 + b), far[j, h, b])

    stages = ("xc", "y", "z")

    def red_start(which, stage, value):
        buf = reds[which].at[stage]
        _, me, _ = group(stages[stage])
        buf[me] = value
        for _, device in others(stages[stage]):
            pltpu.make_async_remote_copy(
                buf.at[me],
                buf.at[me],
                red_send.at[which, stage],
                red_recv.at[which, stage],
                device_id=device,
                device_id_type=MESH,
            ).start()

    def red_finish(which, stage):
        buf = reds[which].at[stage]
        seven = buf.at[pl.ds(0, 7)]
        pltpu.make_async_copy(seven, seven, red_recv.at[which, stage]).wait()
        total = buf[0]
        for i in range(1, 8):
            total = total + buf[i]
        if which == 0:
            largest = buf[0]
            for i in range(1, 8):
                largest = jnp.maximum(largest, buf[i])
            row = lax.broadcasted_iota(jnp.int32, total.shape, 0)
            total = jnp.where(row < 2, total, largest)
        return total

    def inner_products(makers, pairs):
        step = 128

        def body(i, sums):
            rows = pl.ds(pl.multiple_of(i * step, step), step)
            vectors = [make(rows) for make in makers]
            return tuple(
                total + jnp.sum((vectors[a] * vectors[c]).reshape(step // 8, 8, 128), axis=0)
                for total, (a, c) in zip(sums, pairs)
            )

        sums = lax.fori_loop(
            0, ROWS // step, body, tuple(jnp.zeros((8, 128), F32) for _ in pairs)
        )
        return [jnp.sum(total, axis=0, keepdims=True) for total in sums]

    def payload(values, rows):
        pieces = [half for pair in zip(*values) for half in pair]
        if len(pieces) < rows:
            pieces.append(jnp.zeros((rows - len(pieces), 128), F32))
        return jnp.concatenate(pieces, axis=0)

    def largest_of(ref, count):
        def body(i, best):
            return jnp.maximum(best, jnp.max(jnp.abs(ref[i].astype(F32).reshape(48, 8, BLOCK)), axis=0))

        best = lax.fori_loop(0, count, body, jnp.zeros((8, BLOCK), F32))
        return jnp.max(jnp.max(best, axis=0, keepdims=True), axis=1, keepdims=True)

    def wells_start():
        wells[zone] = well_ref[...]
        for _, device in others("zone"):
            pltpu.make_async_remote_copy(
                wells.at[zone],
                wells.at[zone],
                well_send.at[3],
                well_recv.at[3],
                device_id=device,
                device_id_type=MESH,
            ).start()

    def pick_build():
        cells = cell_ref[...]
        for b in range(2):
            for q in range(3):
                row = lax.broadcasted_iota(jnp.int32, (128, 128), 0) + b * 128
                upper, lower = split(jnp.where(row == cells, -coeff_ref[q], 0.0).T)
                columns = pl.ds(b * BLOCK + q * 128, 128)
                pick[pl.ds(0, 128), columns] = upper
                pick[pl.ds(128, 128), columns] = lower

    def lows_build():
        fifteen = wells.at[pl.ds(0, 15)]
        pltpu.make_async_copy(fifteen, fifteen, well_recv.at[3]).wait()

        def body(i, carry):
            ids = wells[i]
            code = ((ids >> 7) << 3) + (ids & 7)
            row = lax.broadcasted_iota(jnp.int32, (128, 128), 0)
            columns = pl.ds(pl.multiple_of(i * 128, 128), 128)
            lows[:, columns] = jnp.where(row == code, 1.0, 0.0).astype(BF)
            chunk = jnp.broadcast_to((ids >> 3) & 15, (16, 128))
            for k in range(16):
                hots[i, pl.ds(k * 16, 16)] = jnp.where(chunk == k, 1.0, 0.0).astype(BF)
            return carry

        lax.fori_loop(0, 16, body, 0)

    def contrib_start(j):
        upper = jnp.concatenate([high[j, 0], high[j, 1]], axis=1)
        lower = jnp.concatenate([low[j, 0], low[j, 1]], axis=1)
        value = dot(pick[...], upper)
        value = value[:128] + value[128:] + dot(pick[pl.ds(0, 128)], lower)
        contrib[j] = jnp.concatenate([value[:, :128].T, value[:, 128:].T], axis=0).reshape(16, 16, 128)
        spread[j, zone] = contrib[j, zone]
        for slot, device in others("zone"):
            pltpu.make_async_remote_copy(
                contrib.at[j, slot],
                spread.at[j, zone],
                well_send.at[j],
                well_recv.at[j],
                device_id=device,
                device_id_type=MESH,
            ).start()

    def dense_start(j):
        fifteen = spread.at[j, pl.ds(0, 15)]
        pltpu.make_async_copy(fifteen, fifteen, well_recv.at[j]).wait()

        def body(i, carry):
            upper, lower = split(spread[j, i])
            columns = pl.ds(pl.multiple_of(i * 128, 128), 128)
            hot = hots[i]
            placed[pl.ds(0, 256), columns] = jnp.concatenate([upper] * 16, axis=0) * hot
            placed[pl.ds(256, 256), columns] = jnp.concatenate([lower] * 16, axis=0) * hot
            return carry

        lax.fori_loop(0, 16, body, 0)
        total = lax.dot_general(
            placed[...], lows[...], (((1,), (1,)), ((), ())), preferred_element_type=F32
        )
        dense[j] = (total[:256] + total[256:]).reshape(32, 8, 128)
        partial[j, sub] = dense[j, sub]
        for slot, device in others("sub"):
            pltpu.make_async_remote_copy(
                dense.at[j, slot],
                partial.at[j, sub],
                well_send.at[4 + j],
                well_recv.at[4 + j],
                device_id=device,
                device_id_type=MESH,
            ).start()

    def dense_finish(j):
        most = partial.at[j, pl.ds(0, 31)]
        pltpu.make_async_copy(most, most, well_recv.at[4 + j]).wait()
        total = partial[j, 0]
        for i in range(1, 32):
            total = total + partial[j, i]
        _, me, _ = group("pair")
        final[j, me] = total
        for _, device in others("pair"):
            pltpu.make_async_remote_copy(
                final.at[j, me],
                final.at[j, me],
                well_send.at[7 + j],
                well_recv.at[7 + j],
                device_id=device,
                device_id_type=MESH,
            ).start()

    def own_wells(j):
        most = final.at[j, pl.ds(0, 31)]
        pltpu.make_async_copy(most, most, well_recv.at[7 + j]).wait()
        gathered = final[j].reshape(R, 128)
        turned[...] = jnp.concatenate([gathered[:128].T, gathered[128:].T], axis=1)
        eight = turned[pl.ds(pl.multiple_of(zone * 8, 8), 8)]
        return jnp.where(lax.rem(sub, 2) == 0, eight[:4], eight[4:])

    pick_build()
    loads[0].wait()
    loads[1].wait()
    for b in range(2):
        found = dot(pre[b], rhs[pl.ds(b * BLOCK, BLOCK)])
        for h in range(2):
            keep(0, h, b, found[:, h * 128 : h * 128 + 128])

    def right_side(h):
        return lambda rows: rhs[rows, pl.ds(h * 128, 128)].astype(F32)

    square = [inner_products([right_side(h)], [(0, 0)])[0] for h in range(2)]
    loads[2].wait()
    size_pre = largest_of(pre, 2)
    size_op = jnp.maximum(largest_of(diag, 2), OFF_MOST)
    pl.semaphore_wait(barrier, greeted)
    red_start(
        0,
        0,
        jnp.concatenate(
            square
            + [
                jnp.broadcast_to(size_pre, (1, 128)),
                jnp.broadcast_to(size_op, (1, 128)),
                jnp.zeros((4, 128), F32),
            ],
            axis=0,
        ),
    )
    halo_start(0, 0)
    halo_start(0, 1)
    wells_start()
    contrib_start(0)
    loads[3].wait()
    local_products(0, 0)
    local_products(0, 1)
    red_start(0, 1, red_finish(0, 0))
    for h in range(2):
        halo_products(0, h)
        precondition(1, h, None)
        halo_start(1, h)

    contrib_start(1)
    local_products(1, 0)
    red_start(0, 2, red_finish(0, 1))
    local_products(1, 1)
    lows_build()
    dense_start(0)
    scales = []

    def scale_of(h):
        def make():
            if not scales:
                sizes = red_finish(0, 2)
                norm = jnp.sqrt(sizes[:2])
                shrink = 1.0 / (sizes[2:3] * sizes[3:4])
                scales.extend([norm, shrink, 1.0 / norm])
            norm, shrink, inverse = scales
            return shrink * inverse[h : h + 1]

        return make

    for h in range(2):
        halo_products(1, h)
        precondition(2, h, scale_of(h))
        halo_start(2, h)

    norm, shrink, inverse = scales

    def makers(h, count):
        scale0 = inverse[h : h + 1]
        scale1 = shrink * scale0
        return [
            lambda rows: rhs[rows, pl.ds(h * 128, 128)].astype(F32) * scale0,
            lambda rows: image[0, h, rows] * scale0,
            lambda rows: image[1, h, rows] * scale1,
            lambda rows: image[2, h, rows] * shrink,
        ][:count]

    contrib_start(2)
    early = [
        inner_products(makers(h, 3), [(0, 1), (0, 2), (1, 1), (1, 2), (2, 2)]) for h in range(2)
    ]
    red_start(1, 0, payload(early, 16))
    local_products(2, 0)
    local_products(2, 1)
    dense_start(1)
    red_start(1, 1, red_finish(1, 0))
    dense_finish(0)
    late = []
    for h in range(2):
        halo_products(2, h)
        late.append(inner_products(makers(h, 4), [(0, 3), (1, 3), (2, 3), (3, 3)]))
    red_start(2, 0, payload(late, 8))
    dense_start(2)
    red_start(2, 1, red_finish(2, 0))
    red_start(1, 2, red_finish(1, 1))
    dense_finish(1)
    owned = [own_wells(0)]
    red_start(2, 2, red_finish(2, 1))
    head = red_finish(1, 2)
    g0, g1, m00, m01, m11 = [head[2 * i : 2 * i + 2] for i in range(5)]
    dense_finish(2)
    owned.append(own_wells(1))
    tail = red_finish(2, 2)
    g2, m02, m12, m22 = [tail[2 * i : 2 * i + 2] for i in range(4)]

    e01 = m01 / m00
    e02 = m02 / m00
    p11 = m11 - e01 * m01
    p12 = m12 - e01 * m02
    e12 = p12 / p11
    p22 = m22 - e02 * m02 - e12 * p12
    f0 = g0
    f1 = g1 - e01 * f0
    f2 = g2 - e02 * f0 - e12 * f1
    c2 = f2 / p22
    c1 = f1 / p11 - e12 * c2
    c0 = f0 / m00 - e01 * c1 - e02 * c2
    coeffs = [c0, c1 * shrink, c2 * shrink * norm]

    stores = []
    for part in range(4):
        rows = pl.ds(part * 192, 192)
        for h in range(2):
            total = coeffs[0][h : h + 1] * search[0, h, rows]
            for j in range(1, ITERS):
                total = total + coeffs[j][h : h + 1] * search[j, h, rows]
            out[rows, pl.ds(h * 128, 128)] = total
        store = pltpu.make_async_copy(out.at[rows], adj_hbm.at[rows], store_sem.at[part])
        store.start()
        stores.append(store)

    owned.append(own_wells(2))
    gradient = jnp.zeros((4, R), F32)
    for j in range(ITERS):
        wide = jnp.concatenate([coeffs[j][0:1], coeffs[j][1:2]], axis=1)
        gradient = gradient + wide * owned[j]
    grad_ref[...] = gradient

    for store in stores:
        store.wait()
    for j in range(ITERS):
        for h in range(2):
            for b in range(2):
                for kind in (SLOW, SIDE, FAST):
                    copy, sends, _ = halo(j, h, kind, b)
                    guarded(sends, copy.wait_send)
    for which in range(3):
        for stage in range(3):
            seven = reds[which].at[stage, pl.ds(0, 7)]
            pltpu.make_async_copy(seven, seven, red_send.at[which, stage]).wait()
    for j in range(ITERS):
        fifteen = spread.at[j, pl.ds(0, 15)]
        pltpu.make_async_copy(fifteen, fifteen, well_send.at[j]).wait()
        most = partial.at[j, pl.ds(0, 31)]
        pltpu.make_async_copy(most, most, well_send.at[4 + j]).wait()
        most = final.at[j, pl.ds(0, 31)]
        pltpu.make_async_copy(most, most, well_send.at[7 + j]).wait()
    fifteen = wells.at[pl.ds(0, 15)]
    pltpu.make_async_copy(fifteen, fifteen, well_send.at[3]).wait()


def shards(
    diag_blocks,
    precond_blocks,
    offdiag_blocks,
    offdiag_col,
    slot_live,
    adjoint_rhs,
    perf_cell,
    perf_well,
    perf_coeff,
):
    any_spec = pl.BlockSpec(memory_space=pl.ANY)
    smem = pl.BlockSpec(memory_space=pltpu.SMEM)
    vmem = pl.BlockSpec(memory_space=pltpu.VMEM)
    dma = pltpu.SemaphoreType.DMA
    adjoint, gradient = pl.pallas_call(
        kernel,
        out_shape=(
            jax.ShapeDtypeStruct((ROWS, R), F32),
            jax.ShapeDtypeStruct((4, R), F32),
        ),
        in_specs=[any_spec] * 4 + [smem] * 2 + [vmem] * 3,
        out_specs=(any_spec, vmem),
        scratch_shapes=[
            pltpu.VMEM((2, BLOCK, BLOCK), BF),
            pltpu.VMEM((2, BLOCK, BLOCK), BF),
            pltpu.VMEM((8, BLOCK, BLOCK), BF),
            pltpu.VMEM((ROWS, R), BF),
            pltpu.VMEM((ITERS, 2, ROWS, 128), F32),
            pltpu.VMEM((ITERS, 2, ROWS, 128), F32),
            pltpu.VMEM((ITERS, 2, ROWS, 128), BF),
            pltpu.VMEM((ITERS, 2, ROWS, 128), BF),
            pltpu.VMEM((ITERS, 2, 2, BLOCK, 128), BF),
            pltpu.VMEM((ITERS, 2, 2, BLOCK, 128), BF),
            pltpu.VMEM((ITERS, 2, 2, BLOCK, 128), BF),
            pltpu.VMEM((3, 8, 8, 128), F32),
            pltpu.VMEM((3, 8, 16, 128), F32),
            pltpu.VMEM((3, 8, 8, 128), F32),
            pltpu.VMEM((256, ROWS), BF),
            pltpu.VMEM((16, 1, 128), jnp.int32),
            pltpu.VMEM((128, 2048), BF),
            pltpu.VMEM((16, 256, 128), BF),
            pltpu.VMEM((ITERS, 16, 16, 128), F32),
            pltpu.VMEM((ITERS, 16, 16, 128), F32),
            pltpu.VMEM((512, 2048), BF),
            pltpu.VMEM((ITERS, 32, 8, 128), F32),
            pltpu.VMEM((ITERS, 32, 8, 128), F32),
            pltpu.VMEM((ITERS, 32, 8, 128), F32),
            pltpu.VMEM((128, R), F32),
            pltpu.VMEM((ROWS, R), F32),
            dma((4,)),
            dma((ITERS, 2, 6)),
            dma((ITERS, 2, 6)),
            dma((3, 3)),
            dma((3, 3)),
            dma((10,)),
            dma((10,)),
            dma((4,)),
        ],
        compiler_params=pltpu.CompilerParams(
            collective_id=0, has_side_effects=True, vmem_limit_bytes=60 * 1024 * 1024
        ),
        name="adjoint_solve",
    )(
        diag_blocks.reshape(2, BLOCK, BLOCK),
        precond_blocks.reshape(2, BLOCK, BLOCK),
        offdiag_blocks.reshape(8, BLOCK, BLOCK),
        adjoint_rhs.reshape(ROWS, R),
        offdiag_col.reshape(2, 4),
        slot_live.reshape(2, 4),
        perf_cell.reshape(1, 128),
        perf_well.reshape(1, 128),
        perf_coeff.reshape(3, 1, 128),
    )
    return adjoint.reshape(1, 1, 2, BLOCK, R), gradient


def solution(mesh):
    placed = (
        P("zone", "sub", None, None, None),
        P("zone", "sub", None, None, None),
        P("zone", "sub", None, None, None, None),
        P("zone", "sub", None, None),
        P("zone", "sub", None, None),
        P("zone", "sub", None, None, None),
        P("zone", "sub", None),
        P("zone", "sub", None),
        P("zone", "sub", None, None),
    )
    return jax.shard_map(
        shards,
        mesh=mesh,
        in_specs=placed,
        out_specs=(P("zone", "sub", None, None, None), P(("zone", "sub"), None)),
        check_vma=False,
    )
```

time: 78.8 us -> 67.1 us (0.85)
  local copies, waits for them, and re-layouts: 9.61 us -> 3.33 us
  Pallas kernels: 68.2 us -> 62.9 us
    unnamed x19 -> x2, local copies, waits for them, and re-layouts: 9.61 us -> 3.33 us
    pallas_call x1, Pallas kernels: 68.2 us -> 62.9 us  [shards(): pl.pallas_call(kernel, out_shape=(jax.ShapeDtypeStruct((ROWS, R), F32), j...]
where the time goes in v2:
time: 67.1 us; the launch traced here: 66.9 us
  Pallas kernels  62.9 us (94%)
  local copies, waits for them, and re-layouts  3.33 us (5%)
    pallas_call x1, Pallas kernels, shards(): pl.pallas_call(kernel, out_shape=(jax.ShapeDtypeStruct((ROWS, R), F32), j...  62.9 us
    unnamed x2, local copies, waits for them, and re-layouts  3.33 us

profile of v2, /device:TPU:1, one launch (start us, length us, event | category | flops | bytes accessed | tf_op | source)
XLA Modules:
  0.0 66.9 jit_solution(2132764208366228975)
XLA Ops:
  0.6 62.9 %adjoint_solve.1 = (f32[768,256]{1,0:T(8,128)}, f32[4,256]{1,0:T(4,128)}) custom-call(bf16[2,384,384]{2,1,0:T(8,128)(2,1)} %bitcast.12, bf16[2,384,384]{2,1,0:T(8,128)(2,1)} %bitcast.13, bf16[8,384,384]{2,1,0:T(8,128)(2,1)} %bitcast.10, bf16[768,256]{1,0:T(8,128)(2,1)} %bitcast.14, s32[2,4]{1,0:T(2,128)} %bitcast.16, s32[2,4]{1,0:T(2,128)} %bitcast.17, ...), custom_call_target="tpu_custom_call" | custom-call | tf_op jit(solution)/shard_map/adjoint_solve/pallas_call | solution.py:575
  63.6 2.1 %copy.13 = f32[1,1,2,384,256]{4,3,2,1,0:T(8,128)} copy(f32[1,1,2,384,256]{4,3,2,1,0:T(8,128)} %bitcast.11) | data formatting | bytes 1572864
  65.6 1.3 %copy.14 = f32[4,256]{1,0:T(4,128)} copy(f32[4,256]{1,0:T(4,128)} %get-tuple-element.9) | data formatting | bytes 8192

commit v3 on v2

--- a/solution.py
+++ b/solution.py
@@ -25,27 +25,38 @@
     return zone, sub, zone // 2, lax.rem(zone, 2), sub // 4, lax.rem(sub, 4)
 
 
-def group(name):
-    zone, sub, y, core, z, x = place()
-    if name == "xc":
-        return 8, core * 4 + x, lambda i: (y * 2 + i // 4, z * 4 + lax.rem(i, 4))
-    if name == "y":
-        return 8, y, lambda i: (i * 2 + core, sub)
-    if name == "z":
-        return 8, z, lambda i: (zone, i * 4 + x)
-    if name == "zone":
-        return 16, zone, lambda i: (i, sub)
-    if name == "sub":
-        return 32, sub, lambda i: (zone, i)
-    pair = sub // 2 * 2
-    return 32, zone * 2 + lax.rem(sub, 2), lambda i: (i // 2, pair + lax.rem(i, 2))
-
-
-def others(name):
-    count, me, at = group(name)
-    for step in range(1, count):
-        slot = lax.rem(me + step, count)
-        yield slot, at(slot)
+def layout():
+    _, _, y, core, z, x = place()
+    twice = [2 * lax.rem(y + step, 8) for step in range(8)]
+    cores = [core, 1 - core]
+    layers = [lax.rem(z + step, 8) for step in range(8)]
+    across = [lax.rem(x + step, 4) for step in range(4)]
+    pair = [lax.rem(x, 2), 1 - lax.rem(x, 2)]
+    aside = x - pair[0]
+    one, two, four, eight = [(0,), (0, 1), range(4), range(8)]
+    spans = {
+        "xc": (one, two, one, four, lambda q, c, l, a: c * 4 + a),
+        "y": (eight, one, one, one, lambda q, c, l, a: q // 2),
+        "z": (one, one, eight, one, lambda q, c, l, a: l),
+        "zone": (eight, two, one, one, lambda q, c, l, a: q + c),
+        "sub": (one, one, eight, four, lambda q, c, l, a: l * 4 + a),
+        "pair": (eight, two, one, two, lambda q, c, l, a: (q + c) * 2 + a),
+    }
+    groups = {}
+    for name, (dys, dcs, dzs, dxs, slot_of) in spans.items():
+        found = []
+        for dy in dys:
+            for dc in dcs:
+                for dz in dzs:
+                    for dx in dxs:
+                        hops = min(dy, 8 - dy) + min(dz, 8 - dz) + min(dx, 4 - dx) + 0.4 * dc
+                        a = pair[dx] if name == "pair" else across[dx]
+                        slot = slot_of(twice[dy], cores[dc], layers[dz], a)
+                        where = aside + a if name == "pair" else a
+                        device = (twice[dy] + cores[dc], layers[dz] * 4 + where)
+                        found.append((hops, slot, device))
+        groups[name] = (found[0][1], [(slot, device) for hops, slot, device in sorted(found[1:], key=lambda e: -e[0])])
+    return groups
 
 
 def split(value):
@@ -62,13 +73,18 @@
     pre_hbm,
     off_hbm,
     rhs_hbm,
+    col_hbm,
+    live_hbm,
+    cell_hbm,
+    well_hbm,
+    coeff_hbm,
+    adj_ref,
+    grad_ref,
     col_ref,
     live_ref,
     cell_ref,
     well_ref,
     coeff_ref,
-    adj_hbm,
-    grad_ref,
     diag,
     pre,
     off,
@@ -94,7 +110,6 @@
     partial,
     final,
     turned,
-    out,
     load_sem,
     halo_send,
     halo_recv,
@@ -102,15 +117,28 @@
     red_recv,
     well_send,
     well_recv,
-    store_sem,
 ):
     zone, sub, y, core, z, x = place()
     reds = (red0, red1, red2)
+    groups = layout()
+
+    def others(name):
+        return groups[name][1]
 
     loads = [
         pltpu.make_async_copy(src, dst, load_sem.at[i])
         for i, (src, dst) in enumerate(
-            ((pre_hbm, pre), (rhs_hbm, rhs), (diag_hbm, diag), (off_hbm, off))
+            (
+                (pre_hbm, pre),
+                (rhs_hbm, rhs),
+                (diag_hbm, diag),
+                (off_hbm, off),
+                (cell_hbm, cell_ref),
+                (coeff_hbm, coeff_ref),
+                (well_hbm, well_ref),
+                (col_hbm, col_ref),
+                (live_hbm, live_ref),
+            )
         )
     ]
     for load in loads:
@@ -228,7 +256,7 @@
 
     def red_start(which, stage, value):
         buf = reds[which].at[stage]
-        _, me, _ = group(stages[stage])
+        me = groups[stages[stage]][0]
         buf[me] = value
         for _, device in others(stages[stage]):
             pltpu.make_async_remote_copy(
@@ -374,7 +402,7 @@
         total = partial[j, 0]
         for i in range(1, 32):
             total = total + partial[j, i]
-        _, me, _ = group("pair")
+        me = groups["pair"][0]
         final[j, me] = total
         for _, device in others("pair"):
             pltpu.make_async_remote_copy(
@@ -394,6 +422,8 @@
         eight = turned[pl.ds(pl.multiple_of(zone * 8, 8), 8)]
         return jnp.where(lax.rem(sub, 2) == 0, eight[:4], eight[4:])
 
+    loads[4].wait()
+    loads[5].wait()
     pick_build()
     loads[0].wait()
     loads[1].wait()
@@ -425,9 +455,12 @@
     )
     halo_start(0, 0)
     halo_start(0, 1)
+    loads[6].wait()
     wells_start()
     contrib_start(0)
     loads[3].wait()
+    loads[7].wait()
+    loads[8].wait()
     local_products(0, 0)
     local_products(0, 1)
     red_start(0, 1, red_finish(0, 0))
@@ -515,17 +548,13 @@
     c0 = f0 / m00 - e01 * c1 - e02 * c2
     coeffs = [c0, c1 * shrink, c2 * shrink * norm]
 
-    stores = []
     for part in range(4):
         rows = pl.ds(part * 192, 192)
         for h in range(2):
             total = coeffs[0][h : h + 1] * search[0, h, rows]
             for j in range(1, ITERS):
                 total = total + coeffs[j][h : h + 1] * search[j, h, rows]
-            out[rows, pl.ds(h * 128, 128)] = total
-        store = pltpu.make_async_copy(out.at[rows], adj_hbm.at[rows], store_sem.at[part])
-        store.start()
-        stores.append(store)
+            adj_ref[rows, pl.ds(h * 128, 128)] = total
 
     owned.append(own_wells(2))
     gradient = jnp.zeros((4, R), F32)
@@ -534,8 +563,6 @@
         gradient = gradient + wide * owned[j]
     grad_ref[...] = gradient
 
-    for store in stores:
-        store.wait()
     for j in range(ITERS):
         for h in range(2):
             for b in range(2):
@@ -569,18 +596,22 @@
     perf_coeff,
 ):
     any_spec = pl.BlockSpec(memory_space=pl.ANY)
-    smem = pl.BlockSpec(memory_space=pltpu.SMEM)
     vmem = pl.BlockSpec(memory_space=pltpu.VMEM)
     dma = pltpu.SemaphoreType.DMA
     adjoint, gradient = pl.pallas_call(
         kernel,
         out_shape=(
-            jax.ShapeDtypeStruct((ROWS, R), F32),
-            jax.ShapeDtypeStruct((4, R), F32),
+            pltpu.VMEM((ROWS, R), F32),
+            pltpu.VMEM((4, R), F32),
         ),
-        in_specs=[any_spec] * 4 + [smem] * 2 + [vmem] * 3,
-        out_specs=(any_spec, vmem),
+        in_specs=[any_spec] * 9,
+        out_specs=(vmem, vmem),
         scratch_shapes=[
+            pltpu.SMEM((2, 4), jnp.int32),
+            pltpu.SMEM((2, 4), jnp.int32),
+            pltpu.VMEM((1, 128), jnp.int32),
+            pltpu.VMEM((1, 128), jnp.int32),
+            pltpu.VMEM((3, 1, 128), F32),
             pltpu.VMEM((2, BLOCK, BLOCK), BF),
             pltpu.VMEM((2, BLOCK, BLOCK), BF),
             pltpu.VMEM((8, BLOCK, BLOCK), BF),
@@ -606,15 +637,13 @@
             pltpu.VMEM((ITERS, 32, 8, 128), F32),
             pltpu.VMEM((ITERS, 32, 8, 128), F32),
             pltpu.VMEM((128, R), F32),
-            pltpu.VMEM((ROWS, R), F32),
-            dma((4,)),
+            dma((9,)),
             dma((ITERS, 2, 6)),
             dma((ITERS, 2, 6)),
             dma((3, 3)),
             dma((3, 3)),
             dma((10,)),
             dma((10,)),
-            dma((4,)),
         ],
         compiler_params=pltpu.CompilerParams(
             collective_id=0, has_side_effects=True, vmem_limit_bytes=60 * 1024 * 1024

time: 67.1 us -> 62.4 us (0.930)
  Pallas kernels: 62.9 us -> 60.1 us
  local copies, waits for them, and re-layouts: 3.33 us -> 1.47 us
    pallas_call x1, Pallas kernels: 62.9 us -> 60.1 us  [shards(): pl.pallas_call(kernel, out_shape=(pltpu.VMEM((ROWS, R), F32), pltpu.VMEM(...]
    unnamed x2, local copies, waits for them, and re-layouts: 3.33 us -> 1.47 us
where the time goes in v3:
time: 62.4 us; the launch traced here: 62.2 us
  Pallas kernels  60.1 us (96%)
  local copies, waits for them, and re-layouts  1.47 us (2%)
  between operations  0.64 us (1%)
    pallas_call x1, Pallas kernels, shards(): pl.pallas_call(kernel, out_shape=(pltpu.VMEM((ROWS, R), F32), pltpu.VMEM(...  60.1 us
    unnamed x2, local copies, waits for them, and re-layouts  1.47 us

profile of v3, /device:TPU:1, one launch (start us, length us, event | category | flops | bytes accessed | tf_op | source)
XLA Modules:
  0.0 62.2 jit_solution(17631102061326393871)
XLA Ops:
  0.6 60.1 %adjoint_solve.1 = (f32[768,256]{1,0:T(8,128)S(1)}, f32[4,256]{1,0:T(4,128)S(1)}) custom-call(bf16[2,384,384]{2,1,0:T(8,128)(2,1)} %bitcast.12, bf16[2,384,384]{2,1,0:T(8,128)(2,1)} %bitcast.13, bf16[8,384,384]{2,1,0:T(8,128)(2,1)} %bitcast.11, bf16[768,256]{1,0:T(8,128)(2,1)} %bitcast.14, s32[2,4]{1,0:T(2,128)} %bitcast.16, s32[2,4]{1,0:T(2,128)} %bitcast.17, ...), custom_call_target="tpu_custom_call" | custom-call | tf_op jit(solution)/shard_map/adjoint_solve/pallas_call | solution.py:601
  60.7 0.9 %copy.13 = f32[1,1,2,384,256]{4,3,2,1,0:T(8,128)} copy(f32[1,1,2,384,256]{4,3,2,1,0:T(8,128)S(1)} %bitcast.10) | data formatting | bytes 1572864
  61.6 0.6 copy.14

commit v4 on v3

--- a/solution.py
+++ b/solution.py
@@ -15,8 +15,8 @@
 R = 256
 ITERS = 3
 OFF_MOST = 0.09375
+ALPHA = 2.0**-12
 FAST, SLOW, SIDE = 0, 2, 4
-RED_ROWS = (8, 16, 8)
 
 
 def place():
@@ -96,7 +96,8 @@
     near,
     far,
     side,
-    red0,
+    size0,
+    size1,
     red1,
     red2,
     pick,
@@ -119,7 +120,8 @@
     well_recv,
 ):
     zone, sub, y, core, z, x = place()
-    reds = (red0, red1, red2)
+    sizes = (size0, size1)
+    reds = (red1, red2)
     groups = layout()
 
     def others(name):
@@ -275,12 +277,31 @@
         total = buf[0]
         for i in range(1, 8):
             total = total + buf[i]
-        if which == 0:
-            largest = buf[0]
-            for i in range(1, 8):
-                largest = jnp.maximum(largest, buf[i])
-            row = lax.broadcasted_iota(jnp.int32, total.shape, 0)
-            total = jnp.where(row < 2, total, largest)
+        return total
+
+    def size_start(stage, value):
+        name = ("zone", "sub")[stage]
+        buf = sizes[stage]
+        me = groups[name][0]
+        buf[me] = value
+        for _, device in others(name):
+            pltpu.make_async_remote_copy(
+                buf.at[me],
+                buf.at[me],
+                red_send.at[2, stage],
+                red_recv.at[2, stage],
+                device_id=device,
+                device_id_type=MESH,
+            ).start()
+
+    def size_finish(stage):
+        buf = sizes[stage]
+        count = buf.shape[0]
+        rest = buf.at[pl.ds(0, count - 1)]
+        pltpu.make_async_copy(rest, rest, red_recv.at[2, stage]).wait()
+        total = buf[0]
+        for i in range(1, count):
+            total = jnp.maximum(total, buf[i])
         return total
 
     def inner_products(makers, pairs):
@@ -432,27 +453,12 @@
         for h in range(2):
             keep(0, h, b, found[:, h * 128 : h * 128 + 128])
 
-    def right_side(h):
-        return lambda rows: rhs[rows, pl.ds(h * 128, 128)].astype(F32)
-
-    square = [inner_products([right_side(h)], [(0, 0)])[0] for h in range(2)]
     loads[2].wait()
     size_pre = largest_of(pre, 2)
     size_op = jnp.maximum(largest_of(diag, 2), OFF_MOST)
     pl.semaphore_wait(barrier, greeted)
-    red_start(
-        0,
-        0,
-        jnp.concatenate(
-            square
-            + [
-                jnp.broadcast_to(size_pre, (1, 128)),
-                jnp.broadcast_to(size_op, (1, 128)),
-                jnp.zeros((4, 128), F32),
-            ],
-            axis=0,
-        ),
-    )
+    lane = lax.broadcasted_iota(jnp.int32, (1, 128), 1)
+    size_start(0, jnp.where(lane < 64, size_pre, size_op))
     halo_start(0, 0)
     halo_start(0, 1)
     loads[6].wait()
@@ -463,7 +469,7 @@
     loads[8].wait()
     local_products(0, 0)
     local_products(0, 1)
-    red_start(0, 1, red_finish(0, 0))
+    size_start(1, size_finish(0))
     for h in range(2):
         halo_products(0, h)
         precondition(1, h, None)
@@ -471,69 +477,63 @@
 
     contrib_start(1)
     local_products(1, 0)
-    red_start(0, 2, red_finish(0, 1))
     local_products(1, 1)
     lows_build()
     dense_start(0)
     scales = []
 
-    def scale_of(h):
-        def make():
-            if not scales:
-                sizes = red_finish(0, 2)
-                norm = jnp.sqrt(sizes[:2])
-                shrink = 1.0 / (sizes[2:3] * sizes[3:4])
-                scales.extend([norm, shrink, 1.0 / norm])
-            norm, shrink, inverse = scales
-            return shrink * inverse[h : h + 1]
-
-        return make
+    def scale_of():
+        if not scales:
+            largest = size_finish(1)
+            scales.append(1.0 / (largest[:, 0:1] * largest[:, 64:65]))
+        return scales[0] * ALPHA
 
     for h in range(2):
         halo_products(1, h)
-        precondition(2, h, scale_of(h))
+        precondition(2, h, scale_of)
         halo_start(2, h)
 
-    norm, shrink, inverse = scales
+    shrink = scales[0]
 
     def makers(h, count):
-        scale0 = inverse[h : h + 1]
-        scale1 = shrink * scale0
         return [
-            lambda rows: rhs[rows, pl.ds(h * 128, 128)].astype(F32) * scale0,
-            lambda rows: image[0, h, rows] * scale0,
-            lambda rows: image[1, h, rows] * scale1,
+            lambda rows: rhs[rows, pl.ds(h * 128, 128)].astype(F32) * ALPHA,
+            lambda rows: image[0, h, rows] * ALPHA,
+            lambda rows: image[1, h, rows] * (shrink * ALPHA),
             lambda rows: image[2, h, rows] * shrink,
         ][:count]
 
     contrib_start(2)
     early = [
-        inner_products(makers(h, 3), [(0, 1), (0, 2), (1, 1), (1, 2), (2, 2)]) for h in range(2)
+        inner_products(makers(h, 3), [(0, 0), (0, 1), (0, 2), (1, 1), (1, 2), (2, 2)]) for h in range(2)
     ]
-    red_start(1, 0, payload(early, 16))
+    red_start(0, 0, payload(early, 16))
     local_products(2, 0)
     local_products(2, 1)
     dense_start(1)
-    red_start(1, 1, red_finish(1, 0))
-    dense_finish(0)
     late = []
     for h in range(2):
         halo_products(2, h)
+        if h == 0:
+            red_start(0, 1, red_finish(0, 0))
+            dense_finish(0)
         late.append(inner_products(makers(h, 4), [(0, 3), (1, 3), (2, 3), (3, 3)]))
-    red_start(2, 0, payload(late, 8))
+    red_start(1, 0, payload(late, 8))
     dense_start(2)
-    red_start(2, 1, red_finish(2, 0))
-    red_start(1, 2, red_finish(1, 1))
+    red_start(1, 1, red_finish(1, 0))
+    red_start(0, 2, red_finish(0, 1))
     dense_finish(1)
     owned = [own_wells(0)]
-    red_start(2, 2, red_finish(2, 1))
-    head = red_finish(1, 2)
-    g0, g1, m00, m01, m11 = [head[2 * i : 2 * i + 2] for i in range(5)]
+    red_start(1, 2, red_finish(1, 1))
+    head = red_finish(0, 2)
+    square, g0, g1, m00, m01, m11 = [head[2 * i : 2 * i + 2] for i in range(6)]
     dense_finish(2)
     owned.append(own_wells(1))
-    tail = red_finish(2, 2)
+    tail = red_finish(1, 2)
     g2, m02, m12, m22 = [tail[2 * i : 2 * i + 2] for i in range(4)]
 
+    norm = jnp.sqrt(square)
+    g0, g1, g2 = [inner / norm for inner in (g0, g1, g2)]
     e01 = m01 / m00
     e02 = m02 / m00
     p11 = m11 - e01 * m01
@@ -546,7 +546,7 @@
     c2 = f2 / p22
     c1 = f1 / p11 - e12 * c2
     c0 = f0 / m00 - e01 * c1 - e02 * c2
-    coeffs = [c0, c1 * shrink, c2 * shrink * norm]
+    coeffs = [norm * c0, norm * (c1 * shrink), norm * (c2 * shrink) * (1.0 / ALPHA)]
 
     for part in range(4):
         rows = pl.ds(part * 192, 192)
@@ -569,7 +569,10 @@
                 for kind in (SLOW, SIDE, FAST):
                     copy, sends, _ = halo(j, h, kind, b)
                     guarded(sends, copy.wait_send)
-    for which in range(3):
+    for stage in range(2):
+        rest = sizes[stage].at[pl.ds(0, sizes[stage].shape[0] - 1)]
+        pltpu.make_async_copy(rest, rest, red_send.at[2, stage]).wait()
+    for which in range(2):
         for stage in range(3):
             seven = reds[which].at[stage, pl.ds(0, 7)]
             pltpu.make_async_copy(seven, seven, red_send.at[which, stage]).wait()
@@ -623,7 +626,8 @@
             pltpu.VMEM((ITERS, 2, 2, BLOCK, 128), BF),
             pltpu.VMEM((ITERS, 2, 2, BLOCK, 128), BF),
             pltpu.VMEM((ITERS, 2, 2, BLOCK, 128), BF),
-            pltpu.VMEM((3, 8, 8, 128), F32),
+            pltpu.VMEM((16, 1, 128), F32),
+            pltpu.VMEM((32, 1, 128), F32),
             pltpu.VMEM((3, 8, 16, 128), F32),
             pltpu.VMEM((3, 8, 8, 128), F32),
             pltpu.VMEM((256, ROWS), BF),

time: 62.4 us -> 60.5 us (0.970)
  Pallas kernels: 60.1 us -> 58.2 us
    pallas_call x1, Pallas kernels: 60.1 us -> 58.2 us  [shards(): pl.pallas_call(kernel, out_shape=(pltpu.VMEM((ROWS, R), F32), pltpu.VMEM(...]
where the time goes in v4:
time: 60.5 us; the launch traced here: 60.3 us
  Pallas kernels  58.2 us (96%)
  local copies, waits for them, and re-layouts  1.47 us (2%)
  between operations  0.64 us (1%)
    pallas_call x1, Pallas kernels, shards(): pl.pallas_call(kernel, out_shape=(pltpu.VMEM((ROWS, R), F32), pltpu.VMEM(...  58.2 us
    unnamed x2, local copies, waits for them, and re-layouts  1.47 us

profile of v4, /device:TPU:1, one launch (start us, length us, event | category | flops | bytes accessed | tf_op | source)
XLA Modules:
  0.0 60.3 jit_solution(13217019814088172146)
XLA Ops:
  0.6 58.2 %adjoint_solve.1 = (f32[768,256]{1,0:T(8,128)S(1)}, f32[4,256]{1,0:T(4,128)S(1)}) custom-call(bf16[2,384,384]{2,1,0:T(8,128)(2,1)} %bitcast.12, bf16[2,384,384]{2,1,0:T(8,128)(2,1)} %bitcast.13, bf16[8,384,384]{2,1,0:T(8,128)(2,1)} %bitcast.11, bf16[768,256]{1,0:T(8,128)(2,1)} %bitcast.14, s32[2,4]{1,0:T(2,128)} %bitcast.16, s32[2,4]{1,0:T(2,128)} %bitcast.17, ...), custom_call_target="tpu_custom_call" | custom-call | tf_op jit(solution)/shard_map/adjoint_solve/pallas_call | solution.py:604
  58.9 0.9 %copy.13 = f32[1,1,2,384,256]{4,3,2,1,0:T(8,128)} copy(f32[1,1,2,384,256]{4,3,2,1,0:T(8,128)S(1)} %bitcast.10) | data formatting | bytes 1572864
  59.7 0.6 copy.14

commit v5 on v4

--- a/solution.py
+++ b/solution.py
@@ -468,8 +468,8 @@
     loads[7].wait()
     loads[8].wait()
     local_products(0, 0)
+    size_start(1, size_finish(0))
     local_products(0, 1)
-    size_start(1, size_finish(0))
     for h in range(2):
         halo_products(0, h)
         precondition(1, h, None)
@@ -523,8 +523,8 @@
     red_start(1, 1, red_finish(1, 0))
     red_start(0, 2, red_finish(0, 1))
     dense_finish(1)
+    red_start(1, 2, red_finish(1, 1))
     owned = [own_wells(0)]
-    red_start(1, 2, red_finish(1, 1))
     head = red_finish(0, 2)
     square, g0, g1, m00, m01, m11 = [head[2 * i : 2 * i + 2] for i in range(6)]
     dense_finish(2)

time: 60.5 us -> 60.6 us (level)
  no operation moved by 1% of the time
where the time goes in v5:
time: 60.6 us; the launch traced here: 60.5 us
  Pallas kernels  58.3 us (96%)
  local copies, waits for them, and re-layouts  1.47 us (2%)
  between operations  0.64 us (1%)
    pallas_call x1, Pallas kernels, shards(): pl.pallas_call(kernel, out_shape=(pltpu.VMEM((ROWS, R), F32), pltpu.VMEM(...  58.3 us
    unnamed x2, local copies, waits for them, and re-layouts  1.47 us

profile of v5, /device:TPU:1, one launch (start us, length us, event | category | flops | bytes accessed | tf_op | source)
XLA Modules:
  0.0 60.5 jit_solution(533885678200889674)
XLA Ops:
  0.6 58.3 %adjoint_solve.1 = (f32[768,256]{1,0:T(8,128)S(1)}, f32[4,256]{1,0:T(4,128)S(1)}) custom-call(bf16[2,384,384]{2,1,0:T(8,128)(2,1)} %bitcast.12, bf16[2,384,384]{2,1,0:T(8,128)(2,1)} %bitcast.13, bf16[8,384,384]{2,1,0:T(8,128)(2,1)} %bitcast.11, bf16[768,256]{1,0:T(8,128)(2,1)} %bitcast.14, s32[2,4]{1,0:T(2,128)} %bitcast.16, s32[2,4]{1,0:T(2,128)} %bitcast.17, ...), custom_call_target="tpu_custom_call" | custom-call | tf_op jit(solution)/shard_map/adjoint_solve/pallas_call | solution.py:604
  59.0 0.9 %copy.13 = f32[1,1,2,384,256]{4,3,2,1,0:T(8,128)} copy(f32[1,1,2,384,256]{4,3,2,1,0:T(8,128)S(1)} %bitcast.10) | data formatting | bytes 1572864
  59.9 0.6 copy.14
